TPU v7x, 256 devices: a whole 4x4x8 slice. The times are simulated.
256 devices in a mesh: row: 32 (over y, x, core), col: 8 (over z).
Axes of the slice: x: 4, y: 4, z: 8, core: 2. Of those that a mesh axis runs over, the one named last changes fastest.
Arguments:
- cov: float32 [1, 32, 256, 4, 8, 256], P(None, 'row', None, None, 'col'), may hold values from -0.4 to 48, as said below
- noise: float32 [], replicated, may hold values from 0.5 to 2
Outputs:
- factor: float32 [1, 32, 256, 2, 256], P(None, 'row')
- trailing: float32 [1, 32, 256, 4, 8, 256], P(None, 'row', None, None, 'col')
Inputs may be any that keep to these rules, and one draw needn't show every extreme that they name: cov is symmetric and A0 is positive definite; its Schur complements after one and two panels stay positive definite.
All inputs are finite; a program needn't handle non-finite values.
Results may differ from a plain program's by a relative error of at most 0.00017.
Values sent between devices are 32-bit elements; how exact they have to be, the bound alone decides.
A program may use at most 64 MiB of HBM per device.

v0:
```python
import jax
import jax.numpy as jnp
from jax import lax
from jax.sharding import PartitionSpec as P


def broadcast(value, axis, root):
    mine = lax.axis_index(axis) == root
    return lax.psum(jnp.where(mine, value, jnp.zeros_like(value)), axis)


def solve_panel(lower, column, grow, step_index):
    tiles, width, _ = column.shape
    flat = column.reshape(tiles * width, width)
    solved = lax.linalg.triangular_solve(lower, flat, left_side=False, lower=True, transpose_a=True)
    solved = solved.reshape(tiles, width, width)
    below = grow[:, None, None] < step_index
    onto = grow[:, None, None] == step_index
    return jnp.where(below, jnp.float32(0.0), jnp.where(onto, lower[None], solved))


def factor_panel(mat, step_index, grow):
    rows = lax.axis_size("row")
    cols = lax.axis_size("col")
    kr_k = step_index // rows
    kc_k = step_index // cols
    column = mat[:, :, kc_k, :]
    tile = broadcast(column[kr_k], "row", step_index % rows)
    lower = jnp.linalg.cholesky(tile)
    solved = solve_panel(lower, column, grow, step_index)
    return broadcast(solved, "col", step_index % cols)


def mirror_panel(lrow, kc_count):
    rows = lax.axis_size("row")
    cols = lax.axis_size("col")
    here = lax.axis_index("col")
    width = lrow.shape[1]

    def one_tile(kc, gathered):
        target = kc * cols + here
        piece = lax.dynamic_index_in_dim(lrow, target // rows, 0, keepdims=False)
        got = broadcast(piece, "row", target % rows)
        return lax.dynamic_update_index_in_dim(gathered, got, kc, 0)

    start = jnp.zeros((kc_count, width, width), jnp.float32)
    return lax.fori_loop(0, kc_count, one_tile, start)


def apply_update(block, lrow, lcol):
    return block - jnp.einsum("aik,bjk->aibj", lrow, lcol, precision=lax.Precision.HIGHEST)


def body(cov, noise):
    rows = lax.axis_size("row")
    cols = lax.axis_size("col")
    mat = cov[:, 0, :, :, 0, :]
    kr_count, width, kc_count, _ = mat.shape
    grow = jnp.arange(kr_count, dtype=jnp.int32) * rows + lax.axis_index("row")
    gcol = jnp.arange(kc_count, dtype=jnp.int32) * cols + lax.axis_index("col")
    same = (grow[:, None] == gcol[None, :]).astype(jnp.float32)
    identity = jnp.eye(width, dtype=jnp.float32)
    mat = mat + noise * same[:, None, :, None] * identity[None, :, None, :]
    lrow_first = factor_panel(mat, 0, grow)
    lcol_first = mirror_panel(lrow_first, kc_count)
    mat = apply_update(mat, lrow_first, lcol_first)
    lrow_second = factor_panel(mat, 1, grow)
    lcol_second = mirror_panel(lrow_second, kc_count)
    mat = apply_update(mat, lrow_second, lcol_second)
    keep = (grow[:, None] >= 2) & (gcol[None, :] >= 2)
    trailing = jnp.where(keep[:, None, :, None], mat, jnp.float32(0.0))
    trailing = trailing.reshape(kr_count, 1, width, kc_count, 1, width)
    factor = jnp.stack([lrow_first, lrow_second], axis=2).reshape(kr_count, 1, width, 2, width)
    return (factor, trailing)


def solution(mesh):
    return jax.shard_map(
        body,
        mesh=mesh,
        in_specs=(P(None, "row", None, None, "col", None), P()),
        out_specs=(P(None, "row", None, None, None), P(None, "row", None, None, "col", None)),
        check_vma=False,
    )
```

profile of v0, /device:TPU:41, one launch (start us, length us, event | category | flops | bytes accessed | tf_op | source)
XLA Modules:
  0.0 1458.5 jit_solution(6509051167401511709)
XLA Ops:
  7.9 2.3 copy.4
  10.3 0.8 broadcast_select_fusion.3
  11.1 114.2 %all-reduce.8.cloned.1.call-done = f32[256,256]{0,1:T(8,128)} async-done(((f32[256,256]{0,1:T(8,128)}), f32[256,256]{0,1:T(8,128)}) %all-reduce.8.cloned.1.call-update) | async-done | bytes 262160 | tf_op jit(solution)/shard_map/psum | solution.py:9
  125.4 1.1 copy.5
  126.6 11.7 cholesky.130
  138.4 9.8 custom-call.13
  148.7 11.7 cholesky.147
  163.0 4.5 while.36
  163.8 1.4 dynamic-slice.12
  165.9 1.4 dynamic-slice.12
  167.5 19.7 %custom-call.14 = f32[2,128,128]{1,2,0:T(8,128)S(1)} custom-call(f32[2,128,128]{2,1,0:T(8,128)S(1)} %get-tuple-element.242), custom_call_target="InvertDiagBlocksLowerTriangular" | custom-call | tf_op jit(solution)/shard_map/triangular_solve/custom-call.0 | solution.py:15
  188.1 0.8 fusion.5
  188.9 67.8 %all-reduce.10.cloned.1.call-done = f32[1,256,256]{1,2,0:T(8,128)} async-done(((f32[1,256,256]{1,2,0:T(8,128)}), f32[1,256,256]{1,2,0:T(8,128)}) %all-reduce.10.cloned.1.call-update) | async-done | bytes 262160 | tf_op jit(solution)/shard_map/psum | solution.py:9
  256.7 1.1 copy.11
  257.9 469.6 %while.34 = (s32[]{:T(128)}, f32[4,256,256]{2,1,0:T(8,128)S(1)}, s32[]{:T(128)}, f32[1,256,256]{2,1,0:T(8,128)S(1)}, s32[]{:T(128)}, /*index=5*/u32[]{:T(128)}, ...) while((s32[]{:T(128)}, f32[4,256,256]{2,1,0:T(8,128)S(1)}, s32[]{:T(128)}, ...), condition=%wide.region_8.11_spmd, body=%wide.region_6.10_spmd.sunk | while | flops 131091 | bytes 2621776 | solution.py:47
  258.7 118.3 %all-reduce.16.cloned.1.call-done = f32[1,256,256]{2,1,0:T(8,128)} async-done(((f32[1,256,256]{2,1,0:T(8,128)}), f32[1,256,256]{2,1,0:T(8,128)}) %all-reduce.16.cloned.1.call-update) | async-done | bytes 262160 | tf_op jit(solution)/shard_map/while/body/eval_jaxpr/psum | solution.py:9
  377.0 1.0 constant_dynamic-update-slice_fusion.8
  378.8 114.7 %all-reduce.16.cloned.1.call-done = f32[1,256,256]{2,1,0:T(8,128)} async-done(((f32[1,256,256]{2,1,0:T(8,128)}), f32[1,256,256]{2,1,0:T(8,128)}) %all-reduce.16.cloned.1.call-update) | async-done | bytes 262160 | tf_op jit(solution)/shard_map/while/body/eval_jaxpr/psum | solution.py:9
  493.5 1.0 constant_dynamic-update-slice_fusion.8
  495.3 114.7 %all-reduce.16.cloned.1.call-done = f32[1,256,256]{2,1,0:T(8,128)} async-done(((f32[1,256,256]{2,1,0:T(8,128)}), f32[1,256,256]{2,1,0:T(8,128)}) %all-reduce.16.cloned.1.call-update) | async-done | bytes 262160 | tf_op jit(solution)/shard_map/while/body/eval_jaxpr/psum | solution.py:9
  610.0 1.0 constant_dynamic-update-slice_fusion.8
  611.8 114.7 %all-reduce.16.cloned.1.call-done = f32[1,256,256]{2,1,0:T(8,128)} async-done(((f32[1,256,256]{2,1,0:T(8,128)}), f32[1,256,256]{2,1,0:T(8,128)}) %all-reduce.16.cloned.1.call-update) | async-done | bytes 262160 | tf_op jit(solution)/shard_map/while/body/eval_jaxpr/psum | solution.py:9
  726.5 1.0 constant_dynamic-update-slice_fusion.8
  727.5 2.0 convolution_subtract_fusion.1
  730.3 113.0 %all-reduce.12.cloned.1.call-done = f32[256,256]{0,1:T(8,128)} async-done(((f32[256,256]{0,1:T(8,128)}), f32[256,256]{0,1:T(8,128)}) %all-reduce.12.cloned.1.call-update) | async-done | bytes 262160 | tf_op jit(solution)/shard_map/psum | solution.py:9
  843.3 1.1 copy.14
  844.5 11.7 cholesky.164
  856.3 9.8 custom-call.15
  866.6 11.7 cholesky.181
  881.3 4.5 while.37
  882.1 1.4 dynamic-slice.14
  884.3 1.4 dynamic-slice.14
  885.8 19.7 %custom-call.16 = f32[2,128,128]{1,2,0:T(8,128)S(1)} custom-call(f32[2,128,128]{2,1,0:T(8,128)S(1)} %get-tuple-element.243), custom_call_target="InvertDiagBlocksLowerTriangular" | custom-call | tf_op jit(solution)/shard_map/triangular_solve/custom-call.0 | solution.py:15
  906.4 0.8 fusion.8
  907.2 67.8 %all-reduce.14.cloned.1.call-done = f32[1,256,256]{1,2,0:T(8,128)} async-done(((f32[1,256,256]{1,2,0:T(8,128)}), f32[1,256,256]{1,2,0:T(8,128)}) %all-reduce.14.cloned.1.call-update) | async-done | bytes 262160 | tf_op jit(solution)/shard_map/psum | solution.py:9
  975.0 1.1 copy.19
  976.2 471.5 %while.35 = (s32[]{:T(128)}, f32[4,256,256]{2,1,0:T(8,128)S(1)}, s32[]{:T(128)}, f32[1,256,256]{2,1,0:T(8,128)S(1)}, s32[]{:T(128)}, /*index=5*/u32[]{:T(128)}, ...) while((s32[]{:T(128)}, f32[4,256,256]{2,1,0:T(8,128)S(1)}, s32[]{:T(128)}, ...), condition=%wide.region_13.16_spmd, body=%wide.region_11.15_spmd.sunk | while | flops 131091 | bytes 2621776 | solution.py:47
  977.0 118.7 %all-reduce.18.cloned.1.call-done = f32[1,256,256]{2,1,0:T(8,128)} async-done(((f32[1,256,256]{2,1,0:T(8,128)}), f32[1,256,256]{2,1,0:T(8,128)}) %all-reduce.18.cloned.1.call-update) | async-done | bytes 262160 | tf_op jit(solution)/shard_map/while/body/eval_jaxpr/psum | solution.py:9
  1095.6 1.0 constant_dynamic-update-slice_fusion.9
  1097.5 115.1 %all-reduce.18.cloned.1.call-done = f32[1,256,256]{2,1,0:T(8,128)} async-done(((f32[1,256,256]{2,1,0:T(8,128)}), f32[1,256,256]{2,1,0:T(8,128)}) %all-reduce.18.cloned.1.call-update) | async-done | bytes 262160 | tf_op jit(solution)/shard_map/while/body/eval_jaxpr/psum | solution.py:9
  1212.6 1.0 constant_dynamic-update-slice_fusion.9
  1214.4 115.4 %all-reduce.18.cloned.1.call-done = f32[1,256,256]{2,1,0:T(8,128)} async-done(((f32[1,256,256]{2,1,0:T(8,128)}), f32[1,256,256]{2,1,0:T(8,128)}) %all-reduce.18.cloned.1.call-update) | async-done | bytes 262160 | tf_op jit(solution)/shard_map/while/body/eval_jaxpr/psum | solution.py:9
  1329.8 1.0 constant_dynamic-update-slice_fusion.9
  1331.6 115.1 %all-reduce.18.cloned.1.call-done = f32[1,256,256]{2,1,0:T(8,128)} async-done(((f32[1,256,256]{2,1,0:T(8,128)}), f32[1,256,256]{2,1,0:T(8,128)}) %all-reduce.18.cloned.1.call-update) | async-done | bytes 262160 | tf_op jit(solution)/shard_map/while/body/eval_jaxpr/psum | solution.py:9
  1446.7 1.0 constant_dynamic-update-slice_fusion.9
  1447.7 1.0 fusion.1
  1448.7 1.9 copy.23
  1450.7 1.0 copy.22
  (103 shorter events, 16.1 us)
Async XLA Ops:
  7.2 118.2 %all-reduce.8.cloned.1.call-start = ((), (), s32[]{:S(2)}) async-start(), calls=%async_computation | async-start | bytes 524288 | tf_op jit(solution)/shard_map/psum | solution.py:9
  11.1 245.6 %all-reduce.10.cloned.1.call-start = ((), (), s32[]{:S(2)}) async-start(), calls=%async_computation.1 | async-start | bytes 524288 | tf_op jit(solution)/shard_map/psum | solution.py:9
  125.4 1.2 copy-start.2
  257.9 119.1 %all-reduce.16.cloned.1.call-start = ((), (), s32[]{:S(2)}) async-start(), calls=%async_computation.4 | async-start | bytes 524288 | tf_op jit(solution)/shard_map/while/body/eval_jaxpr/psum | solution.py:9
  378.0 115.5 %all-reduce.16.cloned.1.call-start = ((), (), s32[]{:S(2)}) async-start(), calls=%async_computation.4 | async-start | bytes 524288 | tf_op jit(solution)/shard_map/while/body/eval_jaxpr/psum | solution.py:9
  494.5 115.5 %all-reduce.16.cloned.1.call-start = ((), (), s32[]{:S(2)}) async-start(), calls=%async_computation.4 | async-start | bytes 524288 | tf_op jit(solution)/shard_map/while/body/eval_jaxpr/psum | solution.py:9
  611.0 115.5 %all-reduce.16.cloned.1.call-start = ((), (), s32[]{:S(2)}) async-start(), calls=%async_computation.4 | async-start | bytes 524288 | tf_op jit(solution)/shard_map/while/body/eval_jaxpr/psum | solution.py:9
  727.5 115.8 %all-reduce.12.cloned.1.call-start = ((), (), s32[]{:S(2)}) async-start(), calls=%async_computation.2 | async-start | bytes 524288 | tf_op jit(solution)/shard_map/psum | solution.py:9
  730.2 244.8 %all-reduce.14.cloned.1.call-start = ((), (), s32[]{:S(2)}) async-start(), calls=%async_computation.3 | async-start | bytes 524288 | tf_op jit(solution)/shard_map/psum | solution.py:9
  843.3 1.2 copy-start.3
  976.1 471.6 %copy-start = (f32[1,256,256]{1,2,0:T(8,128)S(1)}, f32[1,256,256]{1,2,0:T(8,128)}, u32[]{:S(2)}) copy-start(f32[1,256,256]{1,2,0:T(8,128)} %all-reduce.14.cloned.1.call-done) | copy-start | bytes 786436
  976.2 119.5 %all-reduce.18.cloned.1.call-start = ((), (), s32[]{:S(2)}) async-start(), calls=%async_computation.5 | async-start | bytes 524288 | tf_op jit(solution)/shard_map/while/body/eval_jaxpr/psum | solution.py:9
  1096.6 115.9 %all-reduce.18.cloned.1.call-start = ((), (), s32[]{:S(2)}) async-start(), calls=%async_computation.5 | async-start | bytes 524288 | tf_op jit(solution)/shard_map/while/body/eval_jaxpr/psum | solution.py:9
  1213.5 116.2 %all-reduce.18.cloned.1.call-start = ((), (), s32[]{:S(2)}) async-start(), calls=%async_computation.5 | async-start | bytes 524288 | tf_op jit(solution)/shard_map/while/body/eval_jaxpr/psum | solution.py:9
  1330.8 116.0 %all-reduce.18.cloned.1.call-start = ((), (), s32[]{:S(2)}) async-start(), calls=%async_computation.5 | async-start | bytes 524288 | tf_op jit(solution)/shard_map/while/body/eval_jaxpr/psum | solution.py:9
  1448.7 1.9 copy-start.1
Sparse Core Ops, SparseCore 0:
  11.8 113.5 all-reduce.7
  189.0 67.6 all-reduce.9
  262.5 114.4 all-reduce.15
  382.3 111.1 all-reduce.15
  498.8 111.1 all-reduce.15
  615.3 111.1 all-reduce.15
  732.1 111.1 all-reduce.11
  907.3 67.6 all-reduce.13
  981.1 114.4 all-reduce.17
  1101.3 111.2 all-reduce.17
  1218.5 111.2 all-reduce.17
  1335.4 111.2 all-reduce.17
where the time goes:
time: 1460 us
  waiting for transfers between devices  1290 us (88%)
  other arithmetic  117 us (8%)
  local copies, waits for them, and re-layouts  26.8 us (2%)
  between operations  17.8 us (1%)
    psum x12, waiting for transfers between devices, broadcast(): return lax.psum(jnp.where(mine, value, jnp.zeros_like(value)), axis)  1290 us
    another operation x13, other arithmetic, factor_panel(): lower = jnp.linalg.cholesky(tile)  68.6 us
    another operation x5, other arithmetic, solve_panel(): lax.linalg.triangular_solve(lower, flat, left_side=False, lower=True, tra...  39.4 us
  transfers between devices with their start and end apart: 12, of which 12 were waited for; matrix products, arithmetic and copies ran while one was open for 0% of the time, Pallas kernels for 0%

commit v1 on v0

v1 whole, which is shorter than its diff:
```python
import jax
import jax.numpy as jnp
from jax import lax
from jax.experimental import pallas as pl
from jax.experimental.pallas import tpu as pltpu
from jax.sharding import PartitionSpec as P

F32 = jnp.float32
HIGHEST = lax.Precision.HIGHEST
NN = ((1,), (0,))
TN = ((0,), (0,))
NT = ((1,), (1,))
MESH = pl.DeviceIdType.MESH
CHUNKS = 2
WIDTHS = (512, 384, 256, 128)


def dot(a, b, dims):
    return lax.dot_general(a, b, (dims, ((), ())), precision=HIGHEST, preferred_element_type=F32)


def lanes(v, q):
    return jnp.broadcast_to(v[:, q : q + 1], (8, 128))


def sublanes(v, j):
    return jnp.broadcast_to(v[j : j + 1, :], (8, 128))


def factor_inverse_64(tile, group=16):
    count = 8
    per = group // 8
    sub = lax.broadcasted_iota(jnp.int32, (8, 128), 0)
    lane = lax.broadcasted_iota(jnp.int32, (8, 128), 1)
    rows = []
    for h in range(count):
        left = jnp.concatenate([tile[8 * h : 8 * h + 8, :], jnp.zeros((8, 64), F32)], axis=1)
        rows.append(jnp.where(lane < 64, left, (lane - 64 == sub + 8 * h).astype(F32)))
    out = [None] * count
    for g in range(64 // group):
        first = g * per
        col = [[lanes(rows[first + a], group * g + j) for a in range(per)] for j in range(group)]
        later = range(first + per, count)
        mult = {h: [lanes(rows[h], group * g + j) for j in range(group)] for h in later}
        z = [rows[first + a] for a in range(per)]
        w = [jnp.zeros((8, 128), F32) for _ in range(per)]
        pivot = sublanes(col[0][0], 0)
        for j in range(group):
            a0, s0 = j // 8, j % 8
            here = sub == s0
            inv = 1.0 / pivot
            root = lax.rsqrt(pivot)
            if j + 1 < group:
                a1, s1 = (j + 1) // 8, (j + 1) % 8
                cross = sublanes(col[j][a1], s1) * sublanes(col[j + 1][a0], s0)
                pivot = sublanes(col[j + 1][a1], s1) - cross * inv
            line = sublanes(z[a0], s0)
            w[a0] = jnp.where(here, line * root, w[a0])
            line = line * inv
            for a in range(per):
                t = z[a] - col[j][a] * line
                z[a] = jnp.where(here, line, t) if a == a0 else t
            for k in range(j + 1, group):
                m = sublanes(col[k][a0], s0) * inv
                for a in range(per):
                    t = col[k][a] - col[j][a] * m
                    col[k][a] = jnp.where(here, m, t) if a == a0 else t
        for a in range(per):
            out[first + a] = w[a]
        zb = [sublanes(z[j // 8], j % 8) for j in range(group)]
        for h in later:
            t = [mult[h][j] * zb[j] for j in range(group)]
            while len(t) > 1:
                t = [t[i] + t[i + 1] for i in range(0, len(t), 2)]
            rows[h] = rows[h] - t[0]
    return jnp.concatenate(out, axis=0)[:, 64:]


def factor_inverse_128(tile):
    t1 = factor_inverse_64(tile[:64, :64])
    u = dot(t1, tile[:64, 64:], NN)
    rest = tile[64:, 64:] - dot(u, u, TN)
    x = dot(u, t1, TN)
    t2 = factor_inverse_64(rest)
    y = -dot(t2, x, NN)
    top = jnp.concatenate([t1, jnp.zeros((64, 64), F32)], axis=1)
    return jnp.concatenate([top, jnp.concatenate([y, t2], axis=1)], axis=0)


def eye(n):
    return lax.broadcasted_iota(jnp.int32, (n, n), 0) == lax.broadcasted_iota(jnp.int32, (n, n), 1)


def kernel(
    noise_ref, cov_ref, fac_ref, tr_ref,
    s_ref, ar, ac, acc, pr, m0, m1, m2, m3,
    l_a, l_c, l_r, o_sem,
    rc, sc1, sc2, sc3, scs,
    rr, sr1, sr2, rs, ss,
    rmr, rmz, rmi, rms, sm,
):
    r = lax.axis_index("row")
    z = lax.axis_index("col")
    k = lax.rem(r, 2)
    chip = r // 2
    x = lax.rem(chip, 4)
    y = chip // 4
    u = jnp.where(k == 0, x, y)
    v = jnp.where(k == 0, y, x)

    def row_of(uu, vv):
        xx = jnp.where(k == 0, uu, vv)
        yy = jnp.where(k == 0, vv, uu)
        return (yy * 4 + xx) * 2 + k

    sib = r + 1 - 2 * k
    us = [lax.rem(u + d, 4) for d in (1, 2, 3)]
    vs = [lax.rem(v + d, 4) for d in (1, 2, 3)]
    zs = [lax.rem(z + d, 8) for d in range(1, 8)]
    u_row = [row_of(t, v) for t in us]
    v_row = [row_of(u, t) for t in vs]
    msgs = (m0, m1, m2, m3)
    head = (u == 0) & (v == 0)
    edge = v == 0
    is_root = (r == 0) & (z == 0)
    gives = (r == 1) & (z < 2)
    noise = noise_ref[0]
    pending = []

    def copy(src, dst, send, recv, row, col):
        def make():
            return pltpu.make_async_remote_copy(
                src_ref=src, dst_ref=dst, send_sem=send, recv_sem=recv, device_id=(row, col), device_id_type=MESH
            )
        return make

    def send(cond, make):
        if cond is None:
            make().start()
        else:
            @pl.when(cond)
            def _():
                make().start()
        pending.append((cond, make))

    def landed(ref, sem):
        pltpu.make_async_copy(ref, ref, sem).wait()

    def when(cond, fn):
        pl.when(cond)(fn)

    loads_a = [pltpu.make_async_copy(cov_ref.at[0, 0, :, j, 0, :], acc.at[:, pl.ds(256 * j, 256)], l_a.at[j]) for j in range(4)]
    loads_c = [pltpu.make_async_copy(cov_ref.at[0, 0, :, j, 0, :], ac.at[k, j], l_c.at[j]) for j in range(4)]
    load_r = pltpu.make_async_copy(cov_ref.at[0, 0, :, 0, 0, :], ar.at[jnp.minimum(z, 1)], l_r)

    @pl.when(z < 2)
    def _():
        load_r.start()

    @pl.when(head)
    def _():
        for q in loads_c:
            q.start()

    for q in loads_a:
        q.start()

    barrier = pltpu.get_barrier_semaphore()
    for t in u_row + v_row + [sib]:
        pl.semaphore_signal(barrier, 1, device_id=(t, z), device_id_type=MESH)
    for t in zs:
        pl.semaphore_signal(barrier, 1, device_id=(r, t), device_id_type=MESH)

    @pl.when((r == 1) & (z == 1))
    def _():
        pl.semaphore_signal(barrier, 1, device_id=(0, 0), device_id_type=MESH)

    @pl.when(is_root)
    def _():
        pl.semaphore_signal(barrier, 1, device_id=(1, 1), device_id_type=MESH)

    @pl.when(z < 2)
    def _():
        load_r.wait()

    @pl.when((r == 0) & (z != 1))
    def _():
        ar[1] = jnp.zeros((256, 256), F32)

    @pl.when(is_root)
    def _():
        s_ref[0:256, 0:256] = ar[0] + jnp.where(eye(256), noise, 0.0)
        m0[:, 0:128] = factor_inverse_128(s_ref[0:128, 0:128])

    pl.semaphore_wait(barrier, jnp.where(((r == 1) & (z == 1)) | is_root, 15, 14))

    zc = jnp.minimum(z, 1)
    send(gives, copy(ar.at[zc], s_ref.at[pl.ds(256, 256), pl.ds(256 * zc, 256)], ss, rs.at[zc], 0, 0))

    for s in range(2):
        for d in range(7):
            to = (s + d + 1) % 8
            wanted = (z == s) if s == 0 else (z == s) & (r != 0)
            part = pl.ds(32 * to, 32)
            send(wanted, copy(ar.at[s, part], ar.at[s, part], sr1.at[s, d], rr.at[s, to], r, to))

    @pl.when(head)
    def _():
        for q in loads_c:
            q.wait()

    rows = 256 // CHUNKS

    def piece(half, j, ch):
        return ac.at[half, j, pl.ds(rows * ch, rows)]

    for ch in range(CHUNKS):
        for j in (1, 2, 3):
            send(head, copy(piece(k, j, ch), piece(k, j, ch), sc1.at[j - 1, ch], rc.at[k, j, ch], row_of(j, 0), z))
    for ch in range(CHUNKS):
        mine = piece(k, u, ch)

        @pl.when(jnp.logical_not(head))
        def _():
            landed(mine, rc.at[k, u, ch])

        for d in range(3):
            send(edge, copy(mine, mine, sc2.at[d, ch], rc.at[k, u, ch], v_row[d], z))
        for d in range(3):
            wanted = jnp.logical_not((us[d] == 0) & (v == 0))
            send(wanted, copy(mine, mine, sc3.at[d, ch], rc.at[k, u, ch], u_row[d], z))
        send(None, copy(mine, mine, scs.at[0, ch], rc.at[k, u, ch], sib, z))

    for s in range(2):
        flows = None if s == 0 else r != 0
        part = pl.ds(32 * z, 32)
        wait_for = (z != s) if flows is None else (z != s) & flows

        @pl.when(wait_for)
        def _():
            landed(ar.at[s, part], rr.at[s, z])

        for d in range(7):
            wanted = (zs[d] != s) & (z != s)
            if flows is not None:
                wanted = wanted & flows
            send(wanted, copy(ar.at[s, part], ar.at[s, part], sr2.at[s, d], rr.at[s, z], r, zs[d]))
        own = (z == s) if flows is None else (z == s) & flows
        for d in range(7):
            to = (s + d + 1) % 8
            send(own, copy(ar.at[s, pl.ds(32 * s, 32)], ar.at[s, pl.ds(32 * s, 32)], sr2.at[s, d], rr.at[s, s], r, to))

    for ch in range(CHUNKS):
        for d in range(3):
            got = piece(k, us[d], ch)

            @pl.when(jnp.logical_not(head))
            def _():
                landed(got, rc.at[k, us[d], ch])

            send(None, copy(got, got, scs.at[d + 1, ch], rc.at[k, us[d], ch], sib, z))

    early = len(pending)

    def drain(which):
        for cond, make in which:
            if cond is None:
                make().wait_send()
            else:
                pl.when(cond)(lambda make=make: make().wait_send())

    def finish_inputs():
        drain(pending[:early])
        for ch in range(CHUNKS):
            for j in range(4):
                landed(piece(1 - k, j, ch), rc.at[1 - k, j, ch])
        for s in range(2):
            wanted = (z != s) if s == 0 else (z != s) & (r != 0)

            @pl.when(wanted)
            def _():
                for t in zs:
                    landed(ar.at[s, pl.ds(32 * t, 32)], rr.at[s, t])

        for q in loads_a:
            q.wait()
        for j in range(4):
            extra = jnp.where((r // 8 == j) & (lax.rem(r, 8) == z), noise, 0.0)
            sl = slice(256 * j, 256 * j + 256)
            acc[:, sl] = acc[:, sl] + jnp.where(eye(256), extra, 0.0)
        for s in range(2):
            extra = jnp.where(r == s, noise, 0.0)
            ar[s] = ar[s] + jnp.where(eye(256), extra, 0.0)

    def root_step(b):
        o = 128 * b
        if b == 0:
            landed(s_ref.at[pl.ds(256, 256), pl.ds(0, 256)], rs.at[0])
            s_ref[0:256, 256:512] = s_ref[256:512, 0:256].T
        else:
            msgs[b][:, 0:128] = factor_inverse_128(s_ref[o : o + 128, o : o + 128])
        if b == 3:
            return
        right = dot(msgs[b][:, 0:128], s_ref[o : o + 128, o + 128 :], NN)
        msgs[b][:, 128:] = right

    def root_update(b):
        if b == 0:
            landed(s_ref.at[pl.ds(256, 256), pl.ds(256, 256)], rs.at[1])
            s_ref[256:512, 256:512] = s_ref[256:512, 256:512] + jnp.where(eye(256), noise, 0.0)
        for h in range(b + 1, 4):
            left = msgs[b][:, 128 * (h - b) : 128 * (h - b) + 128]
            hl = slice(128 * h, 128 * h + 128)
            s_ref[hl, 128 * h :] = s_ref[hl, 128 * h :] - dot(left, msgs[b][:, 128 * (h - b) :], TN)

    def spread(b):
        m = msgs[b]
        half = m.at[pl.ds(64 * k, 64)]
        other = m.at[pl.ds(64 * (1 - k), 64)]
        at_source = head & (z == 0)
        send(is_root, copy(m.at[pl.ds(64, 64)], m.at[pl.ds(64, 64)], sm.at[b, 0], rmr.at[b], 1, 0))

        @pl.when((r == 1) & (z == 0))
        def _():
            landed(m.at[pl.ds(64, 64)], rmr.at[b])

        def slice_of(t):
            return m.at[pl.ds(64 * k + 8 * t, 8)]

        for t in range(1, 8):
            send(at_source, copy(slice_of(t), slice_of(t), sm.at[b, t], rmz.at[b, t], r, t))
        for t in range(1, 8):
            send(at_source, copy(slice_of(0), slice_of(0), sm.at[b, 7 + t], rmz.at[b, 0], r, t))
        relay = head & (z != 0)

        @pl.when(relay)
        def _():
            landed(slice_of(z), rmz.at[b, z])

        for d in range(7):
            send(relay & (zs[d] != 0), copy(slice_of(z), slice_of(z), sm.at[b, 15 + d], rmz.at[b, z], r, zs[d]))

        @pl.when(relay)
        def _():
            for t in zs:
                landed(slice_of(t), rmz.at[b, t])

        @pl.when(jnp.logical_not(head))
        def _():
            landed(half, rmi.at[b])

        for d in range(3):
            send(head, copy(half, half, sm.at[b, 22 + d], rmi.at[b], u_row[d], z))
        for d in range(3):
            send(edge, copy(half, half, sm.at[b, 25 + d], rmi.at[b], v_row[d], z))
        send(jnp.logical_not((r == 1) & (z == 0)), copy(half, half, sm.at[b, 28], rms.at[b], sib, z))

        @pl.when(jnp.logical_not(is_root))
        def _():
            landed(other, rms.at[b])

    grow = lax.broadcasted_iota(jnp.int32, (256, 128), 0) + 256 * r

    def panel_rows(b, last):
        m = msgs[b]
        part = slice(128 * (b % 2), 128 * (b % 2) + 128)
        p = dot(ar[b // 2, :, part], m[:, 0:128], NT)
        gcol = lax.broadcasted_iota(jnp.int32, (256, 128), 1) + 128 * b
        pr[:, 128 * b : 128 * b + 128] = jnp.where(gcol <= grow, p, 0.0)
        for h in range(b + 1, last):
            hl = slice(128 * (h % 2), 128 * (h % 2) + 128)
            ar[h // 2, :, hl] = ar[h // 2, :, hl] - dot(p, m[:, 128 * (h - b) : 128 * (h - b) + 128], NN)
        return p

    def update(b):
        m = msgs[b]
        p = panel_rows(b, 4)
        rl = slice(128 * (b % 2), 128 * (b % 2) + 128)
        for j in range(4):
            q = dot(m[:, 0:128], ac[b // 2, j, rl, :], NN)
            for h in range(b + 1, 4):
                hl = slice(128 * (h % 2), 128 * (h % 2) + 128)
                left = m[:, 128 * (h - b) : 128 * (h - b) + 128]
                ac[h // 2, j, hl, :] = ac[h // 2, j, hl, :] - dot(left, q, TN)
            sl = slice(256 * j, 256 * j + 256)
            acc[:, sl] = acc[:, sl] - dot(p, q, NN)

    for b in range(4):
        @pl.when(is_root)
        def _():
            root_step(b)

        spread(b)

        @pl.when(is_root)
        def _():
            if b < 3:
                root_update(b)

        @pl.when(jnp.logical_not(is_root))
        def _():
            if b == 0:
                finish_inputs()

        @pl.when(r != 0)
        def _():
            update(b)

    @pl.when(is_root)
    def _():
        finish_inputs()

    @pl.when(r == 0)
    def _():
        panel_rows(0, 2)
        panel_rows(1, 2)
        pr[:, 256:512] = jnp.zeros((256, 256), F32)

    for j in range(4):
        keep = (r >= 2) & (8 * j + z >= 2)
        sl = slice(256 * j, 256 * j + 256)
        acc[:, sl] = jnp.where(keep, acc[:, sl], 0.0)
    outs = [pltpu.make_async_copy(acc.at[:, pl.ds(256 * j, 256)], tr_ref.at[0, 0, :, j, 0, :], o_sem.at[j]) for j in range(4)]
    outs += [pltpu.make_async_copy(pr.at[:, pl.ds(256 * j, 256)], fac_ref.at[0, 0, :, j, :], o_sem.at[4 + j]) for j in range(2)]
    for q in outs:
        q.start()
    drain(pending[early:])
    for q in outs:
        q.wait()


def body(cov, noise):
    anywhere = pl.BlockSpec(memory_space=pl.ANY)
    dma = pltpu.SemaphoreType.DMA
    return pl.pallas_call(
        kernel,
        in_specs=[pl.BlockSpec(memory_space=pltpu.SMEM), anywhere],
        out_specs=[anywhere, anywhere],
        out_shape=[
            jax.ShapeDtypeStruct((1, 1, 256, 2, 256), F32),
            jax.ShapeDtypeStruct((1, 1, 256, 4, 1, 256), F32),
        ],
        scratch_shapes=[
            pltpu.VMEM((512, 512), F32),
            pltpu.VMEM((2, 256, 256), F32),
            pltpu.VMEM((2, 4, 256, 256), F32),
            pltpu.VMEM((256, 1024), F32),
            pltpu.VMEM((256, 512), F32),
        ]
        + [pltpu.VMEM((128, w), F32) for w in WIDTHS]
        + [
            dma((4,)), dma((4,)), dma, dma((6,)),
            dma((2, 4, CHUNKS)), dma((3, CHUNKS)), dma((3, CHUNKS)), dma((3, CHUNKS)), dma((4, CHUNKS)),
            dma((2, 8)), dma((2, 7)), dma((2, 7)), dma((2,)), dma,
            dma((4,)), dma((4, 8)), dma((4,)), dma((4,)), dma((4, 29)),
        ],
        compiler_params=pltpu.CompilerParams(collective_id=0, has_side_effects=True, vmem_limit_bytes=40 * 2**20),
    )(noise.reshape(1), cov)


def solution(mesh):
    return jax.shard_map(
        body,
        mesh=mesh,
        in_specs=(P(None, "row", None, None, "col", None), P()),
        out_specs=(P(None, "row", None, None, None), P(None, "row", None, None, "col", None)),
        check_vma=False,
    )
```

time: 1460 us -> 70.1 us (0.05)
  the two profiles are of different devices: /device:TPU:41 before, /device:TPU:53 now
where the time goes in v1:
time: 70.1 us; the launch traced here: 70 us
  Pallas kernels  65.7 us (94%)
  local copies, waits for them, and re-layouts  2.98 us (4%)
  between operations  1.29 us (2%)
    pallas_call x1, Pallas kernels, body(): pl.pallas_call(kernel, in_specs=[pl.BlockSpec(memory_space=pltpu.SMEM), a...  65.7 us
    unnamed x4, local copies, waits for them, and re-layouts  2.98 us

profile of v1, /device:TPU:53, one launch (start us, length us, event | category | flops | bytes accessed | tf_op | source)
XLA Modules:
  0.0 70.0 jit_solution(2685711379923955308)
XLA Ops:
  1.3 0.0 copy-start
  1.3 1.2 %copy-done = f32[1,1,256,4,1,256]{5,4,3,2,1,0:T(1,128)S(1)} copy-done((f32[1,1,256,4,1,256]{5,4,3,2,1,0:T(1,128)S(1)}, f32[1,1,256,4,1,256]{5,4,3,2,1,0:T(1,128)}, u32[]{:S(2)}) %copy-start) | copy-done | bytes 1048600
  2.5 65.7 %shard_map.41 = (f32[1,1,256,2,256]{4,3,2,1,0:T(2,128)S(1)}, f32[1,1,256,4,1,256]{5,4,3,2,1,0:T(1,128)S(1)}) custom-call(f32[1]{0:T(128)} %bitcast.1.noise_ref, f32[1,1,256,4,1,256]{5,4,3,2,1,0:T(1,128)S(1)} %copy-done), custom_call_target="tpu_custom_call" | custom-call | tf_op jit(solution)/shard_map/pallas_call | solution.py:435
  68.2 0.8 %copy.7 = f32[1,1,256,2,256]{4,3,2,1,0:T(2,128)} copy(f32[1,1,256,2,256]{4,3,2,1,0:T(2,128)S(1)} %get-tuple-element.4) | data formatting | bytes 1048576
  69.0 1.0 %copy.8 = f32[1,1,256,4,1,256]{5,4,3,2,1,0:T(1,128)} copy(f32[1,1,256,4,1,256]{5,4,3,2,1,0:T(1,128)S(1)} %get-tuple-element.5) | data formatting | bytes 2097152
Async XLA Ops:
  1.3 1.2 %copy-start = (f32[1,1,256,4,1,256]{5,4,3,2,1,0:T(1,128)S(1)}, f32[1,1,256,4,1,256]{5,4,3,2,1,0:T(1,128)}, u32[]{:S(2)}) copy-start(f32[1,1,256,4,1,256]{5,4,3,2,1,0:T(1,128)} %cov_ref.1) | copy-start | bytes 3145732

commit v2 on v1

--- a/solution.py
+++ b/solution.py
@@ -6,17 +6,28 @@
 from jax.sharding import PartitionSpec as P
 
 F32 = jnp.float32
-HIGHEST = lax.Precision.HIGHEST
 NN = ((1,), (0,))
 TN = ((0,), (0,))
 NT = ((1,), (1,))
 MESH = pl.DeviceIdType.MESH
-CHUNKS = 2
+CHUNKS = 4
 WIDTHS = (512, 384, 256, 128)
+FAR_FIRST = (10, 9, 11, 6, 14, 2, 8, 5, 7, 13, 15, 1, 3, 4, 12)
+
+
+def split(a):
+    hi = a.astype(jnp.bfloat16)
+    return hi, (a - hi.astype(F32)).astype(jnp.bfloat16)
 
 
 def dot(a, b, dims):
-    return lax.dot_general(a, b, (dims, ((), ())), precision=HIGHEST, preferred_element_type=F32)
+    a = a if isinstance(a, tuple) else split(a)
+    b = b if isinstance(b, tuple) else split(b)
+
+    def one(i, j):
+        return lax.dot_general(a[i], b[j], (dims, ((), ())), preferred_element_type=F32)
+
+    return one(0, 0) + (one(0, 1) + one(1, 0))
 
 
 def lanes(v, q):
@@ -78,9 +89,10 @@
 
 def factor_inverse_128(tile):
     t1 = factor_inverse_64(tile[:64, :64])
-    u = dot(t1, tile[:64, 64:], NN)
+    t1s = split(t1)
+    u = split(dot(t1s, tile[:64, 64:], NN))
     rest = tile[64:, 64:] - dot(u, u, TN)
-    x = dot(u, t1, TN)
+    x = dot(u, t1s, TN)
     t2 = factor_inverse_64(rest)
     y = -dot(t2, x, NN)
     top = jnp.concatenate([t1, jnp.zeros((64, 64), F32)], axis=1)
@@ -92,12 +104,12 @@
 
 
 def kernel(
-    noise_ref, cov_ref, fac_ref, tr_ref,
-    s_ref, ar, ac, acc, pr, m0, m1, m2, m3,
+    noise_hbm, cov_ref, fac_ref, tr_ref,
+    noise_ref, l_n, s_ref, ar, ac, acc, pr, m0, m1, m2, m3,
     l_a, l_c, l_r, o_sem,
     rc, sc1, sc2, sc3, scs,
     rr, sr1, sr2, rs, ss,
-    rmr, rmz, rmi, rms, sm,
+    rmr, rmq, rms, sm,
 ):
     r = lax.axis_index("row")
     z = lax.axis_index("col")
@@ -119,12 +131,14 @@
     zs = [lax.rem(z + d, 8) for d in range(1, 8)]
     u_row = [row_of(t, v) for t in us]
     v_row = [row_of(u, t) for t in vs]
+    chips = [lax.rem(chip + d, 16) for d in range(1, 16)]
+    plane = [2 * t + k for t in chips]
     msgs = (m0, m1, m2, m3)
     head = (u == 0) & (v == 0)
     edge = v == 0
     is_root = (r == 0) & (z == 0)
+    helper = (r == 1) & (z == 0)
     gives = (r == 1) & (z < 2)
-    noise = noise_ref[0]
     pending = []
 
     def copy(src, dst, send, recv, row, col):
@@ -164,9 +178,11 @@
 
     for q in loads_a:
         q.start()
+    load_n = pltpu.make_async_copy(noise_hbm, noise_ref, l_n)
+    load_n.start()
 
     barrier = pltpu.get_barrier_semaphore()
-    for t in u_row + v_row + [sib]:
+    for t in plane + [sib]:
         pl.semaphore_signal(barrier, 1, device_id=(t, z), device_id_type=MESH)
     for t in zs:
         pl.semaphore_signal(barrier, 1, device_id=(r, t), device_id_type=MESH)
@@ -179,6 +195,9 @@
     def _():
         pl.semaphore_signal(barrier, 1, device_id=(1, 1), device_id_type=MESH)
 
+    load_n.wait()
+    noise = noise_ref[0]
+
     @pl.when(z < 2)
     def _():
         load_r.wait()
@@ -192,7 +211,7 @@
         s_ref[0:256, 0:256] = ar[0] + jnp.where(eye(256), noise, 0.0)
         m0[:, 0:128] = factor_inverse_128(s_ref[0:128, 0:128])
 
-    pl.semaphore_wait(barrier, jnp.where(((r == 1) & (z == 1)) | is_root, 15, 14))
+    pl.semaphore_wait(barrier, 23 + jnp.where(((r == 1) & (z == 1)) | is_root, 1, 0))
 
     zc = jnp.minimum(z, 1)
     send(gives, copy(ar.at[zc], s_ref.at[pl.ds(256, 256), pl.ds(256 * zc, 256)], ss, rs.at[zc], 0, 0))
@@ -250,17 +269,16 @@
             to = (s + d + 1) % 8
             send(own, copy(ar.at[s, pl.ds(32 * s, 32)], ar.at[s, pl.ds(32 * s, 32)], sr2.at[s, d], rr.at[s, s], r, to))
 
-    for ch in range(CHUNKS):
-        for d in range(3):
-            got = piece(k, us[d], ch)
-
-            @pl.when(jnp.logical_not(head))
-            def _():
-                landed(got, rc.at[k, us[d], ch])
-
-            send(None, copy(got, got, scs.at[d + 1, ch], rc.at[k, us[d], ch], sib, z))
-
-    early = len(pending)
+    def pass_on():
+        for ch in range(CHUNKS):
+            for d in range(3):
+                got = piece(k, us[d], ch)
+
+                @pl.when(jnp.logical_not(head))
+                def _():
+                    landed(got, rc.at[k, us[d], ch])
+
+                send(None, copy(got, got, scs.at[d + 1, ch], rc.at[k, us[d], ch], sib, z))
 
     def drain(which):
         for cond, make in which:
@@ -270,7 +288,7 @@
                 pl.when(cond)(lambda make=make: make().wait_send())
 
     def finish_inputs():
-        drain(pending[:early])
+        drain(inputs_sent)
         for ch in range(CHUNKS):
             for j in range(4):
                 landed(piece(1 - k, j, ch), rc.at[1 - k, j, ch])
@@ -292,129 +310,147 @@
             extra = jnp.where(r == s, noise, 0.0)
             ar[s] = ar[s] + jnp.where(eye(256), extra, 0.0)
 
+    def left_of(b, h):
+        return msgs[b][:, 128 * (h - b) : 128 * (h - b) + 128]
+
     def root_step(b):
         o = 128 * b
         if b == 0:
             landed(s_ref.at[pl.ds(256, 256), pl.ds(0, 256)], rs.at[0])
             s_ref[0:256, 256:512] = s_ref[256:512, 0:256].T
         else:
-            msgs[b][:, 0:128] = factor_inverse_128(s_ref[o : o + 128, o : o + 128])
+            c = b - 1
+            if c == 0:
+                landed(s_ref.at[pl.ds(256, 256), pl.ds(256, 256)], rs.at[1])
+                s_ref[256:512, 256:512] = s_ref[256:512, 256:512] + jnp.where(eye(256), noise, 0.0)
+            lefts = {h: split(left_of(c, h)) for h in range(b, 4)}
+            tile = s_ref[o : o + 128, o : o + 128] - dot(lefts[b], lefts[b], TN)
+            msgs[b][:, 0:128] = factor_inverse_128(tile)
+            for h in range(b, 4):
+                hl = slice(128 * h, 128 * h + 128)
+                for w in range(max(h, b + 1), 4):
+                    wl = slice(128 * w, 128 * w + 128)
+                    s_ref[hl, wl] = s_ref[hl, wl] - dot(lefts[h], lefts[w], TN)
+        if b < 3:
+            msgs[b][:, 128:] = dot(msgs[b][:, 0:128], s_ref[o : o + 128, o + 128 :], NN)
+
+    inputs_sent = list(pending)
+
+    def share(b, q):
+        return msgs[b].at[pl.ds(pl.multiple_of(8 * q, 8), 8)]
+
+    def carrier(b):
+        return 0 if b == 3 else 1
+
+    def relay(b):
+        m = msgs[b]
+        kb = carrier(b)
+        source = (r == kb) & (z == 0)
+        carries = k == kb
+        if b < 3:
+            send(is_root, copy(m, m, sm.at[b, 0], rmr.at[b], 1, 0))
+
+            @pl.when(helper)
+            def _():
+                landed(m, rmr.at[b])
+
+        for n, q in enumerate(FAR_FIRST):
+            send(source, copy(share(b, q), share(b, q), sm.at[b, 1 + n], rmq.at[b, q], 2 * q + kb, 0))
+        mine = share(b, chip)
+
+        @pl.when(carries & jnp.logical_not(source))
+        def _():
+            landed(mine, rmq.at[b, chip])
+
+        for d in range(7):
+            send(carries & (z == 0), copy(mine, mine, sm.at[b, 16 + d], rmq.at[b, chip], r, zs[d]))
+        for d in range(15):
+            wanted = carries & jnp.logical_not((chips[d] == 0) & (z == 0))
+            send(wanted, copy(mine, mine, sm.at[b, 23 + d], rmq.at[b, chip], plane[d], z))
         if b == 3:
-            return
-        right = dot(msgs[b][:, 0:128], s_ref[o : o + 128, o + 128 :], NN)
-        msgs[b][:, 128:] = right
-
-    def root_update(b):
-        if b == 0:
-            landed(s_ref.at[pl.ds(256, 256), pl.ds(256, 256)], rs.at[1])
-            s_ref[256:512, 256:512] = s_ref[256:512, 256:512] + jnp.where(eye(256), noise, 0.0)
-        for h in range(b + 1, 4):
-            left = msgs[b][:, 128 * (h - b) : 128 * (h - b) + 128]
-            hl = slice(128 * h, 128 * h + 128)
-            s_ref[hl, 128 * h :] = s_ref[hl, 128 * h :] - dot(left, msgs[b][:, 128 * (h - b) :], TN)
-
-    def spread(b):
+            send(source, copy(m, m, sm.at[b, 38], rms.at[b], sib, z))
+
+    def collect(b):
         m = msgs[b]
-        half = m.at[pl.ds(64 * k, 64)]
-        other = m.at[pl.ds(64 * (1 - k), 64)]
-        at_source = head & (z == 0)
-        send(is_root, copy(m.at[pl.ds(64, 64)], m.at[pl.ds(64, 64)], sm.at[b, 0], rmr.at[b], 1, 0))
-
-        @pl.when((r == 1) & (z == 0))
-        def _():
-            landed(m.at[pl.ds(64, 64)], rmr.at[b])
-
-        def slice_of(t):
-            return m.at[pl.ds(64 * k + 8 * t, 8)]
-
-        for t in range(1, 8):
-            send(at_source, copy(slice_of(t), slice_of(t), sm.at[b, t], rmz.at[b, t], r, t))
-        for t in range(1, 8):
-            send(at_source, copy(slice_of(0), slice_of(0), sm.at[b, 7 + t], rmz.at[b, 0], r, t))
-        relay = head & (z != 0)
-
-        @pl.when(relay)
-        def _():
-            landed(slice_of(z), rmz.at[b, z])
-
-        for d in range(7):
-            send(relay & (zs[d] != 0), copy(slice_of(z), slice_of(z), sm.at[b, 15 + d], rmz.at[b, z], r, zs[d]))
-
-        @pl.when(relay)
-        def _():
-            for t in zs:
-                landed(slice_of(t), rmz.at[b, t])
-
-        @pl.when(jnp.logical_not(head))
-        def _():
-            landed(half, rmi.at[b])
-
-        for d in range(3):
-            send(head, copy(half, half, sm.at[b, 22 + d], rmi.at[b], u_row[d], z))
-        for d in range(3):
-            send(edge, copy(half, half, sm.at[b, 25 + d], rmi.at[b], v_row[d], z))
-        send(jnp.logical_not((r == 1) & (z == 0)), copy(half, half, sm.at[b, 28], rms.at[b], sib, z))
-
-        @pl.when(jnp.logical_not(is_root))
-        def _():
-            landed(other, rms.at[b])
+        kb = carrier(b)
+        source = (r == kb) & (z == 0)
+        carries = (k == kb) & jnp.logical_not(source)
+
+        @pl.when(carries)
+        def _():
+            for t in chips:
+                landed(share(b, t), rmq.at[b, t])
+
+        send(carries, copy(m, m, sm.at[b, 38], rms.at[b], sib, z))
+        has = (k == kb) | is_root if b < 3 else k == kb
+
+        @pl.when(jnp.logical_not(has))
+        def _():
+            landed(m, rms.at[b])
 
     grow = lax.broadcasted_iota(jnp.int32, (256, 128), 0) + 256 * r
 
     def panel_rows(b, last):
         m = msgs[b]
         part = slice(128 * (b % 2), 128 * (b % 2) + 128)
-        p = dot(ar[b // 2, :, part], m[:, 0:128], NT)
+        ts = split(m[:, 0:128])
+        p = dot(ar[b // 2, :, part], ts, NT)
         gcol = lax.broadcasted_iota(jnp.int32, (256, 128), 1) + 128 * b
         pr[:, 128 * b : 128 * b + 128] = jnp.where(gcol <= grow, p, 0.0)
+        ps = split(p)
+        lefts = {h: split(left_of(b, h)) for h in range(b + 1, last)}
         for h in range(b + 1, last):
             hl = slice(128 * (h % 2), 128 * (h % 2) + 128)
-            ar[h // 2, :, hl] = ar[h // 2, :, hl] - dot(p, m[:, 128 * (h - b) : 128 * (h - b) + 128], NN)
-        return p
+            ar[h // 2, :, hl] = ar[h // 2, :, hl] - dot(ps, lefts[h], NN)
+        return ts, ps, lefts
 
     def update(b):
-        m = msgs[b]
-        p = panel_rows(b, 4)
+        ts, ps, lefts = panel_rows(b, 4)
         rl = slice(128 * (b % 2), 128 * (b % 2) + 128)
         for j in range(4):
-            q = dot(m[:, 0:128], ac[b // 2, j, rl, :], NN)
+            q = split(dot(ts, ac[b // 2, j, rl, :], NN))
             for h in range(b + 1, 4):
                 hl = slice(128 * (h % 2), 128 * (h % 2) + 128)
-                left = m[:, 128 * (h - b) : 128 * (h - b) + 128]
-                ac[h // 2, j, hl, :] = ac[h // 2, j, hl, :] - dot(left, q, TN)
+                ac[h // 2, j, hl, :] = ac[h // 2, j, hl, :] - dot(lefts[h], q, TN)
             sl = slice(256 * j, 256 * j + 256)
-            acc[:, sl] = acc[:, sl] - dot(p, q, NN)
+            acc[:, sl] = acc[:, sl] - dot(ps, q, NN)
+
+    def step(b):
+        @pl.when(r >= 2)
+        def _():
+            update(b)
 
     for b in range(4):
         @pl.when(is_root)
         def _():
             root_step(b)
 
-        spread(b)
-
-        @pl.when(is_root)
-        def _():
-            if b < 3:
-                root_update(b)
-
-        @pl.when(jnp.logical_not(is_root))
-        def _():
-            if b == 0:
-                finish_inputs()
-
-        @pl.when(r != 0)
-        def _():
-            update(b)
-
-    @pl.when(is_root)
-    def _():
-        finish_inputs()
+        if b < 3:
+            relay(b)
+    relay(3)
+    before = len(pending)
+    pass_on()
+    inputs_sent += pending[before:]
+    collect(0)
+    collect(1)
+    collect(2)
+    finish_inputs()
+    step(0)
+    step(1)
+    step(2)
+    collect(3)
+    step(3)
 
     @pl.when(r == 0)
     def _():
         panel_rows(0, 2)
         panel_rows(1, 2)
         pr[:, 256:512] = jnp.zeros((256, 256), F32)
+
+    @pl.when(r == 1)
+    def _():
+        for b in range(4):
+            panel_rows(b, 4)
 
     for j in range(4):
         keep = (r >= 2) & (8 * j + z >= 2)
@@ -424,7 +460,8 @@
     outs += [pltpu.make_async_copy(pr.at[:, pl.ds(256 * j, 256)], fac_ref.at[0, 0, :, j, :], o_sem.at[4 + j]) for j in range(2)]
     for q in outs:
         q.start()
-    drain(pending[early:])
+    done = {id(e) for e in inputs_sent}
+    drain([e for e in pending if id(e) not in done])
     for q in outs:
         q.wait()
 
@@ -434,13 +471,15 @@
     dma = pltpu.SemaphoreType.DMA
     return pl.pallas_call(
         kernel,
-        in_specs=[pl.BlockSpec(memory_space=pltpu.SMEM), anywhere],
+        in_specs=[anywhere, anywhere],
         out_specs=[anywhere, anywhere],
         out_shape=[
             jax.ShapeDtypeStruct((1, 1, 256, 2, 256), F32),
             jax.ShapeDtypeStruct((1, 1, 256, 4, 1, 256), F32),
         ],
         scratch_shapes=[
+            pltpu.SMEM((1,), F32),
+            dma,
             pltpu.VMEM((512, 512), F32),
             pltpu.VMEM((2, 256, 256), F32),
             pltpu.VMEM((2, 4, 256, 256), F32),
@@ -452,7 +491,7 @@
             dma((4,)), dma((4,)), dma, dma((6,)),
             dma((2, 4, CHUNKS)), dma((3, CHUNKS)), dma((3, CHUNKS)), dma((3, CHUNKS)), dma((4, CHUNKS)),
             dma((2, 8)), dma((2, 7)), dma((2, 7)), dma((2,)), dma,
-            dma((4,)), dma((4, 8)), dma((4,)), dma((4,)), dma((4, 29)),
+            dma((4,)), dma((4, 16)), dma((4,)), dma((4, 39)),
         ],
         compiler_params=pltpu.CompilerParams(collective_id=0, has_side_effects=True, vmem_limit_bytes=40 * 2**20),
     )(noise.reshape(1), cov)

time: 70.1 us -> 59.1 us (0.84)
  the two profiles are of different devices: /device:TPU:53 before, /device:TPU:201 now
where the time goes in v2:
time: 59.1 us; the launch traced here: 59 us
  Pallas kernels  54.7 us (93%)
  local copies, waits for them, and re-layouts  2.98 us (5%)
  between operations  1.29 us (2%)
    pallas_call x1, Pallas kernels, body(): pl.pallas_call(kernel, in_specs=[anywhere, anywhere], out_specs=[anywhere...  54.7 us
    unnamed x4, local copies, waits for them, and re-layouts  2.98 us

profile of v2, /device:TPU:201, one launch (start us, length us, event | category | flops | bytes accessed | tf_op | source)
XLA Modules:
  0.0 59.0 jit_solution(5585085557964789369)
XLA Ops:
  1.3 0.0 copy-start
  1.3 1.2 %copy-done = f32[1,1,256,4,1,256]{5,4,3,2,1,0:T(1,128)S(1)} copy-done((f32[1,1,256,4,1,256]{5,4,3,2,1,0:T(1,128)S(1)}, f32[1,1,256,4,1,256]{5,4,3,2,1,0:T(1,128)}, u32[]{:S(2)}) %copy-start) | copy-done | bytes 1048600
  2.5 54.7 %shard_map.41 = (f32[1,1,256,2,256]{4,3,2,1,0:T(2,128)S(1)}, f32[1,1,256,4,1,256]{5,4,3,2,1,0:T(1,128)S(1)}) custom-call(f32[1]{0:T(128)} %bitcast.1.noise_hbm, f32[1,1,256,4,1,256]{5,4,3,2,1,0:T(1,128)S(1)} %copy-done), custom_call_target="tpu_custom_call" | custom-call | tf_op jit(solution)/shard_map/pallas_call | solution.py:472
  57.2 0.8 %copy.7 = f32[1,1,256,2,256]{4,3,2,1,0:T(2,128)} copy(f32[1,1,256,2,256]{4,3,2,1,0:T(2,128)S(1)} %get-tuple-element.4) | data formatting | bytes 1048576
  58.0 1.0 %copy.8 = f32[1,1,256,4,1,256]{5,4,3,2,1,0:T(1,128)} copy(f32[1,1,256,4,1,256]{5,4,3,2,1,0:T(1,128)S(1)} %get-tuple-element.5) | data formatting | bytes 2097152
Async XLA Ops:
  1.3 1.2 %copy-start = (f32[1,1,256,4,1,256]{5,4,3,2,1,0:T(1,128)S(1)}, f32[1,1,256,4,1,256]{5,4,3,2,1,0:T(1,128)}, u32[]{:S(2)}) copy-start(f32[1,1,256,4,1,256]{5,4,3,2,1,0:T(1,128)} %cov_ref.1) | copy-start | bytes 3145732

commit v3 on v2

--- a/solution.py
+++ b/solution.py
@@ -87,8 +87,9 @@
     return jnp.concatenate(out, axis=0)[:, 64:]
 
 
-def factor_inverse_128(tile):
-    t1 = factor_inverse_64(tile[:64, :64])
+def factor_inverse_128(tile, t1=None):
+    if t1 is None:
+        t1 = factor_inverse_64(tile[:64, :64])
     t1s = split(t1)
     u = split(dot(t1s, tile[:64, 64:], NN))
     rest = tile[64:, 64:] - dot(u, u, TN)
@@ -108,8 +109,8 @@
     noise_ref, l_n, s_ref, ar, ac, acc, pr, m0, m1, m2, m3,
     l_a, l_c, l_r, o_sem,
     rc, sc1, sc2, sc3, scs,
-    rr, sr1, sr2, rs, ss,
-    rmr, rmq, rms, sm,
+    rr, ro, sr1, sr2, rs, ss,
+    rmr, rmo, rmq, rms, sm,
 ):
     r = lax.axis_index("row")
     z = lax.axis_index("col")
@@ -135,7 +136,6 @@
     plane = [2 * t + k for t in chips]
     msgs = (m0, m1, m2, m3)
     head = (u == 0) & (v == 0)
-    edge = v == 0
     is_root = (r == 0) & (z == 0)
     helper = (r == 1) & (z == 0)
     gives = (r == 1) & (z < 2)
@@ -148,14 +148,18 @@
             )
         return make
 
-    def send(cond, make):
+    def start(cond, *makes):
         if cond is None:
-            make().start()
+            for make in makes:
+                make().start()
         else:
             @pl.when(cond)
             def _():
-                make().start()
-        pending.append((cond, make))
+                for make in makes:
+                    make().start()
+
+    def owe(cond, ref, sem):
+        pending.append((cond, ref, sem))
 
     def landed(ref, sem):
         pltpu.make_async_copy(ref, ref, sem).wait()
@@ -209,19 +213,24 @@
     @pl.when(is_root)
     def _():
         s_ref[0:256, 0:256] = ar[0] + jnp.where(eye(256), noise, 0.0)
-        m0[:, 0:128] = factor_inverse_128(s_ref[0:128, 0:128])
+        m0[0:64, 0:64] = factor_inverse_64(s_ref[0:64, 0:64])
 
     pl.semaphore_wait(barrier, 23 + jnp.where(((r == 1) & (z == 1)) | is_root, 1, 0))
 
     zc = jnp.minimum(z, 1)
-    send(gives, copy(ar.at[zc], s_ref.at[pl.ds(256, 256), pl.ds(256 * zc, 256)], ss, rs.at[zc], 0, 0))
-
+    start(gives, copy(ar.at[zc], s_ref.at[pl.ds(256, 256), pl.ds(256 * zc, 256)], ss, rs.at[zc], 0, 0))
+    owe(gives, ar.at[zc], ss)
+
+    owners = (z == 0, (z == 1) & (r != 0))
+    relays = (z != 0, (z != 1) & (r != 0))
     for s in range(2):
+        makes = []
         for d in range(7):
             to = (s + d + 1) % 8
-            wanted = (z == s) if s == 0 else (z == s) & (r != 0)
-            part = pl.ds(32 * to, 32)
-            send(wanted, copy(ar.at[s, part], ar.at[s, part], sr1.at[s, d], rr.at[s, to], r, to))
+            part = ar.at[s, pl.ds(32 * to, 32)]
+            makes.append(copy(part, part, sr1.at[s], ro.at[s], r, to))
+        start(owners[s], *makes)
+        owe(owners[s], ar.at[s, pl.ds(0, 224)], sr1.at[s])
 
     @pl.when(head)
     def _():
@@ -233,41 +242,44 @@
     def piece(half, j, ch):
         return ac.at[half, j, pl.ds(rows * ch, rows)]
 
+    off_head = jnp.logical_not(head)
     for ch in range(CHUNKS):
-        for j in (1, 2, 3):
-            send(head, copy(piece(k, j, ch), piece(k, j, ch), sc1.at[j - 1, ch], rc.at[k, j, ch], row_of(j, 0), z))
+        makes = [copy(piece(k, j, ch), piece(k, j, ch), sc1, rc.at[k, j, ch], row_of(j, 0), z) for j in (2, 1, 3)]
+        start(head, *makes, copy(piece(k, 0, ch), piece(k, 0, ch), sc1, rc.at[k, 0, ch], row_of(0, 2), z))
+    owe(head, ac.at[k], sc1)
+    deals = (v == 0) & (u != 0)
+    again = (v == 2) & (u == 0)
+    skips = (v == 0) & (u != 0)
     for ch in range(CHUNKS):
         mine = piece(k, u, ch)
 
-        @pl.when(jnp.logical_not(head))
+        @pl.when(off_head)
         def _():
             landed(mine, rc.at[k, u, ch])
 
-        for d in range(3):
-            send(edge, copy(mine, mine, sc2.at[d, ch], rc.at[k, u, ch], v_row[d], z))
-        for d in range(3):
-            wanted = jnp.logical_not((us[d] == 0) & (v == 0))
-            send(wanted, copy(mine, mine, sc3.at[d, ch], rc.at[k, u, ch], u_row[d], z))
-        send(None, copy(mine, mine, scs.at[0, ch], rc.at[k, u, ch], sib, z))
+        start(deals, *[copy(mine, mine, sc2, rc.at[k, u, ch], v_row[d], z) for d in (1, 0, 2)])
+        start(again, *[copy(mine, mine, sc2, rc.at[k, u, ch], row_of(0, t), z) for t in (1, 3)])
+        for d in (1, 0, 2):
+            start((v != 0) | (us[d] != 0), copy(mine, mine, sc3, rc.at[k, u, ch], u_row[d], z))
+        start(None, copy(mine, mine, scs, rc.at[k, u, ch], sib, z))
+    owe(deals, ac.at[k, pl.ds(0, 3)], sc2)
+    owe(again, ac.at[k, pl.ds(0, 2)], sc2)
+    owe(skips, ac.at[k, pl.ds(0, 2)], sc3)
+    owe(jnp.logical_not(skips), ac.at[k, pl.ds(0, 3)], sc3)
 
     for s in range(2):
-        flows = None if s == 0 else r != 0
-        part = pl.ds(32 * z, 32)
-        wait_for = (z != s) if flows is None else (z != s) & flows
-
-        @pl.when(wait_for)
-        def _():
-            landed(ar.at[s, part], rr.at[s, z])
-
-        for d in range(7):
-            wanted = (zs[d] != s) & (z != s)
-            if flows is not None:
-                wanted = wanted & flows
-            send(wanted, copy(ar.at[s, part], ar.at[s, part], sr2.at[s, d], rr.at[s, z], r, zs[d]))
-        own = (z == s) if flows is None else (z == s) & flows
-        for d in range(7):
-            to = (s + d + 1) % 8
-            send(own, copy(ar.at[s, pl.ds(32 * s, 32)], ar.at[s, pl.ds(32 * s, 32)], sr2.at[s, d], rr.at[s, s], r, to))
+        part = ar.at[s, pl.ds(32 * z, 32)]
+
+        @pl.when(relays[s])
+        def _():
+            landed(part, ro.at[s])
+            for d in range(7):
+                start(zs[d] != s, copy(part, part, sr2.at[s], rr.at[s], r, zs[d]))
+
+        owe(relays[s], ar.at[s, pl.ds(0, 192)], sr2.at[s])
+        first = ar.at[s, pl.ds(32 * s, 32)]
+        start(owners[s], *[copy(first, first, sr2.at[s], rr.at[s], r, (s + d + 1) % 8) for d in range(7)])
+        owe(owners[s], ar.at[s, pl.ds(0, 224)], sr2.at[s])
 
     def pass_on():
         for ch in range(CHUNKS):
@@ -278,14 +290,15 @@
                 def _():
                     landed(got, rc.at[k, us[d], ch])
 
-                send(None, copy(got, got, scs.at[d + 1, ch], rc.at[k, us[d], ch], sib, z))
+                start(None, copy(got, got, scs, rc.at[k, us[d], ch], sib, z))
+        owe(None, ac.at[k], scs)
 
     def drain(which):
-        for cond, make in which:
+        for cond, ref, sem in which:
             if cond is None:
-                make().wait_send()
+                landed(ref, sem)
             else:
-                pl.when(cond)(lambda make=make: make().wait_send())
+                pl.when(cond)(lambda ref=ref, sem=sem: landed(ref, sem))
 
     def finish_inputs():
         drain(inputs_sent)
@@ -293,12 +306,9 @@
             for j in range(4):
                 landed(piece(1 - k, j, ch), rc.at[1 - k, j, ch])
         for s in range(2):
-            wanted = (z != s) if s == 0 else (z != s) & (r != 0)
-
-            @pl.when(wanted)
+            @pl.when(relays[s])
             def _():
-                for t in zs:
-                    landed(ar.at[s, pl.ds(32 * t, 32)], rr.at[s, t])
+                landed(ar.at[s, pl.ds(0, 224)], rr.at[s])
 
         for q in loads_a:
             q.wait()
@@ -316,6 +326,7 @@
     def root_step(b):
         o = 128 * b
         if b == 0:
+            m0[:, 0:128] = factor_inverse_128(s_ref[0:128, 0:128], m0[0:64, 0:64])
             landed(s_ref.at[pl.ds(256, 256), pl.ds(0, 256)], rs.at[0])
             s_ref[0:256, 256:512] = s_ref[256:512, 0:256].T
         else:
@@ -348,27 +359,38 @@
         source = (r == kb) & (z == 0)
         carries = k == kb
         if b < 3:
-            send(is_root, copy(m, m, sm.at[b, 0], rmr.at[b], 1, 0))
+            start(is_root, copy(m, m, sm.at[b, 0], rmr.at[b], 1, 0))
+            owe(is_root, m, sm.at[b, 0])
 
             @pl.when(helper)
             def _():
                 landed(m, rmr.at[b])
 
-        for n, q in enumerate(FAR_FIRST):
-            send(source, copy(share(b, q), share(b, q), sm.at[b, 1 + n], rmq.at[b, q], 2 * q + kb, 0))
+        start(source, *[copy(share(b, q), share(b, q), sm.at[b, 1], rmo.at[b], 2 * q + kb, 0) for q in FAR_FIRST])
+        owe(source, m.at[pl.ds(0, 120)], sm.at[b, 1])
         mine = share(b, chip)
 
         @pl.when(carries & jnp.logical_not(source))
         def _():
-            landed(mine, rmq.at[b, chip])
-
-        for d in range(7):
-            send(carries & (z == 0), copy(mine, mine, sm.at[b, 16 + d], rmq.at[b, chip], r, zs[d]))
-        for d in range(15):
-            wanted = carries & jnp.logical_not((chips[d] == 0) & (z == 0))
-            send(wanted, copy(mine, mine, sm.at[b, 23 + d], rmq.at[b, chip], plane[d], z))
+            landed(mine, rmo.at[b])
+
+        deal_z = carries & (z == 0)
+        start(deal_z, *[copy(mine, mine, sm.at[b, 2], rmo.at[b], r, zs[d]) for d in range(7)])
+        owe(deal_z, m.at[pl.ds(0, 56)], sm.at[b, 2])
+        full = carries & ((z != 0) | (chip == 0))
+        start(full, *[copy(mine, mine, sm.at[b, 3], rmq.at[b], plane[d], z) for d in range(15)])
+        owe(full, m.at[pl.ds(0, 120)], sm.at[b, 3])
+        short = deal_z & (chip != 0)
+
+        @pl.when(short)
+        def _():
+            for d in range(15):
+                start(chips[d] != 0, copy(mine, mine, sm.at[b, 3], rmq.at[b], plane[d], z))
+
+        owe(short, m.at[pl.ds(0, 112)], sm.at[b, 3])
         if b == 3:
-            send(source, copy(m, m, sm.at[b, 38], rms.at[b], sib, z))
+            start(source, copy(m, m, sm.at[b, 4], rms.at[b], sib, z))
+            owe(source, m, sm.at[b, 4])
 
     def collect(b):
         m = msgs[b]
@@ -378,10 +400,10 @@
 
         @pl.when(carries)
         def _():
-            for t in chips:
-                landed(share(b, t), rmq.at[b, t])
-
-        send(carries, copy(m, m, sm.at[b, 38], rms.at[b], sib, z))
+            landed(m.at[pl.ds(0, 120)], rmq.at[b])
+            copy(m, m, sm.at[b, 4], rms.at[b], sib, z)().start()
+
+        owe(carries, m, sm.at[b, 4])
         has = (k == kb) | is_root if b < 3 else k == kb
 
         @pl.when(jnp.logical_not(has))
@@ -489,9 +511,9 @@
         + [pltpu.VMEM((128, w), F32) for w in WIDTHS]
         + [
             dma((4,)), dma((4,)), dma, dma((6,)),
-            dma((2, 4, CHUNKS)), dma((3, CHUNKS)), dma((3, CHUNKS)), dma((3, CHUNKS)), dma((4, CHUNKS)),
-            dma((2, 8)), dma((2, 7)), dma((2, 7)), dma((2,)), dma,
-            dma((4,)), dma((4, 16)), dma((4,)), dma((4, 39)),
+            dma((2, 4, CHUNKS)), dma, dma, dma, dma,
+            dma((2,)), dma((2,)), dma((2,)), dma((2,)), dma((2,)), dma,
+            dma((4,)), dma((4,)), dma((4,)), dma((4,)), dma((4, 5)),
         ],
         compiler_params=pltpu.CompilerParams(collective_id=0, has_side_effects=True, vmem_limit_bytes=40 * 2**20),
     )(noise.reshape(1), cov)

time: 59.1 us -> 55.5 us (0.939)
  the two profiles are of different devices: /device:TPU:201 before, /device:TPU:231 now
where the time goes in v3:
time: 55.5 us; the launch traced here: 55.3 us
  Pallas kernels  51.1 us (92%)
  local copies, waits for them, and re-layouts  2.98 us (5%)
  between operations  1.29 us (2%)
    pallas_call x1, Pallas kernels, body(): pl.pallas_call(kernel, in_specs=[anywhere, anywhere], out_specs=[anywhere...  51.1 us
    unnamed x4, local copies, waits for them, and re-layouts  2.98 us

profile of v3, /device:TPU:231, one launch (start us, length us, event | category | flops | bytes accessed | tf_op | source)
XLA Modules:
  0.0 55.3 jit_solution(6875366991415816986)
XLA Ops:
  1.3 0.0 copy-start
  1.3 1.2 %copy-done = f32[1,1,256,4,1,256]{5,4,3,2,1,0:T(1,128)S(1)} copy-done((f32[1,1,256,4,1,256]{5,4,3,2,1,0:T(1,128)S(1)}, f32[1,1,256,4,1,256]{5,4,3,2,1,0:T(1,128)}, u32[]{:S(2)}) %copy-start) | copy-done | bytes 1048600
  2.5 51.1 %shard_map.41 = (f32[1,1,256,2,256]{4,3,2,1,0:T(2,128)S(1)}, f32[1,1,256,4,1,256]{5,4,3,2,1,0:T(1,128)S(1)}) custom-call(f32[1]{0:T(128)} %bitcast.1.noise_hbm, f32[1,1,256,4,1,256]{5,4,3,2,1,0:T(1,128)S(1)} %copy-done), custom_call_target="tpu_custom_call" | custom-call | tf_op jit(solution)/shard_map/pallas_call | solution.py:494
  53.6 0.8 %copy.7 = f32[1,1,256,2,256]{4,3,2,1,0:T(2,128)} copy(f32[1,1,256,2,256]{4,3,2,1,0:T(2,128)S(1)} %get-tuple-element.4) | data formatting | bytes 1048576
  54.4 1.0 %copy.8 = f32[1,1,256,4,1,256]{5,4,3,2,1,0:T(1,128)} copy(f32[1,1,256,4,1,256]{5,4,3,2,1,0:T(1,128)S(1)} %get-tuple-element.5) | data formatting | bytes 2097152
Async XLA Ops:
  1.3 1.2 %copy-start = (f32[1,1,256,4,1,256]{5,4,3,2,1,0:T(1,128)S(1)}, f32[1,1,256,4,1,256]{5,4,3,2,1,0:T(1,128)}, u32[]{:S(2)}) copy-start(f32[1,1,256,4,1,256]{5,4,3,2,1,0:T(1,128)} %cov_ref.1) | copy-start | bytes 3145732

commit v4 on v3

--- a/solution.py
+++ b/solution.py
@@ -250,6 +250,20 @@
     deals = (v == 0) & (u != 0)
     again = (v == 2) & (u == 0)
     skips = (v == 0) & (u != 0)
+    for s in range(2):
+        part = ar.at[s, pl.ds(32 * z, 32)]
+
+        @pl.when(relays[s])
+        def _():
+            landed(part, ro.at[s])
+            for d in range(7):
+                start(zs[d] != s, copy(part, part, sr2.at[s], rr.at[s], r, zs[d]))
+
+        owe(relays[s], ar.at[s, pl.ds(0, 192)], sr2.at[s])
+        first = ar.at[s, pl.ds(32 * s, 32)]
+        start(owners[s], *[copy(first, first, sr2.at[s], rr.at[s], r, (s + d + 1) % 8) for d in range(7)])
+        owe(owners[s], ar.at[s, pl.ds(0, 224)], sr2.at[s])
+
     for ch in range(CHUNKS):
         mine = piece(k, u, ch)
 
@@ -266,20 +280,6 @@
     owe(again, ac.at[k, pl.ds(0, 2)], sc2)
     owe(skips, ac.at[k, pl.ds(0, 2)], sc3)
     owe(jnp.logical_not(skips), ac.at[k, pl.ds(0, 3)], sc3)
-
-    for s in range(2):
-        part = ar.at[s, pl.ds(32 * z, 32)]
-
-        @pl.when(relays[s])
-        def _():
-            landed(part, ro.at[s])
-            for d in range(7):
-                start(zs[d] != s, copy(part, part, sr2.at[s], rr.at[s], r, zs[d]))
-
-        owe(relays[s], ar.at[s, pl.ds(0, 192)], sr2.at[s])
-        first = ar.at[s, pl.ds(32 * s, 32)]
-        start(owners[s], *[copy(first, first, sr2.at[s], rr.at[s], r, (s + d + 1) % 8) for d in range(7)])
-        owe(owners[s], ar.at[s, pl.ds(0, 224)], sr2.at[s])
 
     def pass_on():
         for ch in range(CHUNKS):
@@ -410,6 +410,8 @@
         def _():
             landed(m, rms.at[b])
 
+    outs = [pltpu.make_async_copy(acc.at[:, pl.ds(256 * j, 256)], tr_ref.at[0, 0, :, j, 0, :], o_sem.at[j]) for j in range(4)]
+    outs += [pltpu.make_async_copy(pr.at[:, pl.ds(256 * j, 256)], fac_ref.at[0, 0, :, j, :], o_sem.at[4 + j]) for j in range(2)]
     grow = lax.broadcasted_iota(jnp.int32, (256, 128), 0) + 256 * r
 
     def panel_rows(b, last):
@@ -435,7 +437,11 @@
                 hl = slice(128 * (h % 2), 128 * (h % 2) + 128)
                 ac[h // 2, j, hl, :] = ac[h // 2, j, hl, :] - dot(lefts[h], q, TN)
             sl = slice(256 * j, 256 * j + 256)
-            acc[:, sl] = acc[:, sl] - dot(ps, q, NN)
+            new = acc[:, sl] - dot(ps, q, NN)
+            acc[:, sl] = new if b < 3 else jnp.where(8 * j + z >= 2, new, 0.0)
+        if b == 3:
+            for q in outs:
+                q.start()
 
     def step(b):
         @pl.when(r >= 2)
@@ -474,14 +480,12 @@
         for b in range(4):
             panel_rows(b, 4)
 
-    for j in range(4):
-        keep = (r >= 2) & (8 * j + z >= 2)
-        sl = slice(256 * j, 256 * j + 256)
-        acc[:, sl] = jnp.where(keep, acc[:, sl], 0.0)
-    outs = [pltpu.make_async_copy(acc.at[:, pl.ds(256 * j, 256)], tr_ref.at[0, 0, :, j, 0, :], o_sem.at[j]) for j in range(4)]
-    outs += [pltpu.make_async_copy(pr.at[:, pl.ds(256 * j, 256)], fac_ref.at[0, 0, :, j, :], o_sem.at[4 + j]) for j in range(2)]
-    for q in outs:
-        q.start()
+    @pl.when(r < 2)
+    def _():
+        acc[...] = jnp.zeros((256, 1024), F32)
+        for q in outs:
+            q.start()
+
     done = {id(e) for e in inputs_sent}
     drain([e for e in pending if id(e) not in done])
     for q in outs:

time: 55.5 us -> 51.1 us (0.921)
  the two profiles are of different devices: /device:TPU:231 before, /device:TPU:41 now
where the time goes in v4:
time: 51.1 us; the launch traced here: 51 us
  Pallas kernels  46.7 us (91%)
  local copies, waits for them, and re-layouts  2.98 us (6%)
  between operations  1.29 us (3%)
    pallas_call x1, Pallas kernels, body(): pl.pallas_call(kernel, in_specs=[anywhere, anywhere], out_specs=[anywhere...  46.7 us
    unnamed x4, local copies, waits for them, and re-layouts  2.98 us

profile of v4, /device:TPU:41, one launch (start us, length us, event | category | flops | bytes accessed | tf_op | source)
XLA Modules:
  0.0 51.0 jit_solution(15528716234705603964)
XLA Ops:
  1.3 0.0 copy-start
  1.3 1.2 %copy-done = f32[1,1,256,4,1,256]{5,4,3,2,1,0:T(1,128)S(1)} copy-done((f32[1,1,256,4,1,256]{5,4,3,2,1,0:T(1,128)S(1)}, f32[1,1,256,4,1,256]{5,4,3,2,1,0:T(1,128)}, u32[]{:S(2)}) %copy-start) | copy-done | bytes 1048600
  2.5 46.7 %shard_map.41 = (f32[1,1,256,2,256]{4,3,2,1,0:T(2,128)S(1)}, f32[1,1,256,4,1,256]{5,4,3,2,1,0:T(1,128)S(1)}) custom-call(f32[1]{0:T(128)} %bitcast.1.noise_hbm, f32[1,1,256,4,1,256]{5,4,3,2,1,0:T(1,128)S(1)} %copy-done), custom_call_target="tpu_custom_call" | custom-call | tf_op jit(solution)/shard_map/pallas_call | solution.py:498
  49.2 0.8 %copy.7 = f32[1,1,256,2,256]{4,3,2,1,0:T(2,128)} copy(f32[1,1,256,2,256]{4,3,2,1,0:T(2,128)S(1)} %get-tuple-element.4) | data formatting | bytes 1048576
  50.0 1.0 %copy.8 = f32[1,1,256,4,1,256]{5,4,3,2,1,0:T(1,128)} copy(f32[1,1,256,4,1,256]{5,4,3,2,1,0:T(1,128)S(1)} %get-tuple-element.5) | data formatting | bytes 2097152
Async XLA Ops:
  1.3 1.2 %copy-start = (f32[1,1,256,4,1,256]{5,4,3,2,1,0:T(1,128)S(1)}, f32[1,1,256,4,1,256]{5,4,3,2,1,0:T(1,128)}, u32[]{:S(2)}) copy-start(f32[1,1,256,4,1,256]{5,4,3,2,1,0:T(1,128)} %cov_ref.1) | copy-start | bytes 3145732

commit v5 on v4

--- a/solution.py
+++ b/solution.py
@@ -497,7 +497,7 @@
     dma = pltpu.SemaphoreType.DMA
     return pl.pallas_call(
         kernel,
-        in_specs=[anywhere, anywhere],
+        in_specs=[anywhere, pl.BlockSpec(memory_space=pltpu.HBM)],
         out_specs=[anywhere, anywhere],
         out_shape=[
             jax.ShapeDtypeStruct((1, 1, 256, 2, 256), F32),

time: 51.1 us -> 51.1 us (level)
  no operation moved by 1% of the time
where the time goes in v5:
time: 51.1 us; the launch traced here: 51 us
  Pallas kernels  46.7 us (91%)
  local copies, waits for them, and re-layouts  2.98 us (6%)
  between operations  1.29 us (3%)
    pallas_call x1, Pallas kernels, body(): pl.pallas_call(kernel, in_specs=[anywhere, pl.BlockSpec(memory_space=pltp...  46.7 us
    unnamed x4, local copies, waits for them, and re-layouts  2.98 us

profile of v5, /device:TPU:41, one launch (start us, length us, event | category | flops | bytes accessed | tf_op | source)
XLA Modules:
  0.0 51.0 jit_solution(15528716234705603964)
XLA Ops:
  1.3 0.0 copy-start
  1.3 1.2 %copy-done = f32[1,1,256,4,1,256]{5,4,3,2,1,0:T(1,128)S(1)} copy-done((f32[1,1,256,4,1,256]{5,4,3,2,1,0:T(1,128)S(1)}, f32[1,1,256,4,1,256]{5,4,3,2,1,0:T(1,128)}, u32[]{:S(2)}) %copy-start) | copy-done | bytes 1048600
  2.5 46.7 %shard_map.41 = (f32[1,1,256,2,256]{4,3,2,1,0:T(2,128)S(1)}, f32[1,1,256,4,1,256]{5,4,3,2,1,0:T(1,128)S(1)}) custom-call(f32[1]{0:T(128)} %bitcast.1.noise_hbm, f32[1,1,256,4,1,256]{5,4,3,2,1,0:T(1,128)S(1)} %copy-done), custom_call_target="tpu_custom_call" | custom-call | tf_op jit(solution)/shard_map/pallas_call | solution.py:498
  49.2 0.8 %copy.7 = f32[1,1,256,2,256]{4,3,2,1,0:T(2,128)} copy(f32[1,1,256,2,256]{4,3,2,1,0:T(2,128)S(1)} %get-tuple-element.4) | data formatting | bytes 1048576
  50.0 1.0 %copy.8 = f32[1,1,256,4,1,256]{5,4,3,2,1,0:T(1,128)} copy(f32[1,1,256,4,1,256]{5,4,3,2,1,0:T(1,128)S(1)} %get-tuple-element.5) | data formatting | bytes 2097152
Async XLA Ops:
  1.3 1.2 %copy-start = (f32[1,1,256,4,1,256]{5,4,3,2,1,0:T(1,128)S(1)}, f32[1,1,256,4,1,256]{5,4,3,2,1,0:T(1,128)}, u32[]{:S(2)}) copy-start(f32[1,1,256,4,1,256]{5,4,3,2,1,0:T(1,128)} %cov_ref.1) | copy-start | bytes 3145732
